TPU v7x, 128 devices: a whole 4x4x4 slice. The times are simulated.
128 devices in a mesh: node: 64 (over z, y, x), feat: 2 (over core).
Axes of the slice: x: 4, y: 4, z: 4, core: 2. Of those that a mesh axis runs over, the one named last changes fastest.
Arguments:
- features: bfloat16 [327680, 1024], P('node', 'feat'), may hold values from -6 to 6
- upstream: bfloat16 [327680, 1024], P('node', 'feat'), may hold values from -6 to 6
- preact: bfloat16 [327680, 1024], P('node', 'feat'), may hold values from -6 to 6
- adj_tiles: bfloat16 [5120, 128, 128], P('node'), may hold values from 0 to 0.14941406
- tile_source: int32 [5120], P('node'), may hold values from 0 to 119
Outputs:
- weight_grad: float32 [1024, 1024], P('feat', 'node')
All inputs are finite; a program needn't handle non-finite values.
Results may differ from a plain program's by a relative error of at most 0.0022.
Values may be sent and summed in bfloat16 or wider, within the bound.
A program may use at most 256 MiB of HBM per device.

v0:
```python
import jax
import jax.numpy as jnp
from jax import lax
from jax.sharding import PartitionSpec as P


def shifted(shard, axis, by):
    count = lax.axis_size(axis)
    return lax.ppermute(shard, axis, [(i, (i + by) % count) for i in range(count)])


def exact_product(left_full, right_full):
    dims = (((0,), (0,)), ((), ()))
    return lax.dot_general(
        left_full,
        right_full,
        dims,
        precision=lax.Precision.HIGHEST,
        preferred_element_type=jnp.float32,
    )


def local(features, upstream, preact, adj_tiles, tile_source):
    row_count, fslice = features.shape
    hslice = upstream.shape[1]
    tile_size = adj_tiles.shape[1]
    blocks = row_count // tile_size
    tiles_each = adj_tiles.shape[0] // blocks
    grad_out = jnp.where(preact > 0, upstream, jnp.zeros_like(upstream))
    factor = float(row_count * lax.axis_size("node")) ** (-0.5)
    contrib = jnp.einsum(
        "bpds,bdh->bpsh",
        adj_tiles.reshape(blocks, tiles_each, tile_size, tile_size),
        grad_out.reshape(blocks, tile_size, hslice),
        preferred_element_type=jnp.float32,
    )
    contrib = contrib.reshape(blocks * tiles_each, tile_size, hslice)
    buffer = jnp.zeros((3 * blocks, tile_size, hslice), jnp.float32).at[tile_source].add(contrib)
    from_lower = shifted(buffer[2 * blocks :], "node", 1)
    from_upper = shifted(buffer[:blocks], "node", -1)
    summed = (buffer[blocks : 2 * blocks] + from_lower + from_upper).reshape(row_count, hslice)
    feat_full = features.astype(jnp.float32)
    partial_grad = exact_product(feat_full, lax.all_gather(summed, "feat", axis=1, tiled=True))
    totals = lax.psum(partial_grad, "node")
    width = partial_grad.shape[1] // lax.axis_size("node")
    result = lax.dynamic_slice_in_dim(totals, lax.axis_index("node") * width, width, 1)
    return result * factor


def solution(mesh):
    in_specs = (
        P("node", "feat"),
        P("node", "feat"),
        P("node", "feat"),
        P("node", None, None),
        P("node"),
    )
    out_specs = P("feat", "node")
    return jax.shard_map(local, mesh=mesh, in_specs=in_specs, out_specs=out_specs, check_vma=False)
```

profile of v0, /device:TPU:0, one launch (start us, length us, event | category | flops | bytes accessed | tf_op | source)
XLA Modules:
  0.0 566.6 jit_solution(5919715014062591395)
XLA Ops:
  6.5 0.0 copy-start
  6.5 0.0 all-gather.2.cloned.1.call-start
  6.5 0.8 compare_select_fusion.1
  7.3 4.6 compare_select_fusion
  12.0 0.0 copy-done
  12.0 8.6 %fusion.2 = f32[40,512,2,128]{3,1,2,0:T(8,128)} fusion(bf16[40,128,512,1]{2,1,3,0:T(8,128)(2,1)S(1)} %bitcast.19, bf16[40,2,128,128]{3,2,1,0:T(8,128)(2,1)S(1)} %bitcast.16), kind=kOutput, calls=%fused_computation.8 | convolution fusion | flops 1342177280 | bytes 28835840 | tf_op jit(solution)/shard_map/bpds,bdh->bpsh/dot_general | solution.py:31
  20.6 21.4 %copy.8 = f32[80,128,512]{2,1,0:T(8,128)} copy(f32[80,128,512]{1,2,0:T(8,128)} %bitcast.17) | data formatting | bytes 41943040 | tf_op jit(solution)/shard_map/reshape | solution.py:37
  41.9 14.4 %broadcast_in_dim.6 = f32[120,128,512]{2,1,0:T(8,128)} broadcast(f32[]{:T(128)} %constant.9.clone.1), dimensions={} | broadcast | bytes 31457284 | tf_op jit(solution)/shard_map/broadcast_in_dim | solution.py:38
  56.3 46.3 %scatter_fusion = f32[120,128,512]{2,1,0:T(8,128)} fusion(f32[120,128,512]{2,1,0:T(8,128)} %broadcast_in_dim.6, s32[80]{0:T(128)S(1)} %compare_select_fusion.1, f32[80,128,512]{2,1,0:T(8,128)} %copy.8), kind=kCustom, calls=%fused_computation | custom fusion | flops 5242880 | bytes 62914880 | tf_op jit(solution)/shard_map/scatter-add | solution.py:38
  102.6 13.3 %fusion.1 = (f32[40,128,512]{2,1,0:T(8,128)S(1)}, f32[40,128,512]{2,1,0:T(8,128)}) fusion(f32[120,128,512]{2,1,0:T(8,128)} %scatter_fusion), kind=kLoop, calls=%fused_computation.7 | loop fusion | bytes 41943040 | tf_op jit(solution)/shard_map/slice | solution.py:39
  116.0 8.6 %collective-permute-start.1 = (f32[40,128,512]{2,1,0:T(8,128)}, f32[40,128,512]{2,1,0:T(8,128)S(1)}, u32[]{:S(2)}, u32[]{:S(2)}) collective-permute-start(f32[40,128,512]{2,1,0:T(8,128)} %get-tuple-element.6), channel_id=1, source_target_pairs={{0,126},{2,0},{4,2},{6,4},{8,6},{10,8},{12,10},{14,12},{16,14},{18... | collective-permute-start | bytes 31457288 | tf_op jit(solution)/shard_map/ppermute | solution.py:9
  124.6 0.0 collective-permute-start
  124.6 225.0 %collective-permute-done.1 = f32[40,128,512]{2,1,0:T(8,128)S(1)} collective-permute-done((f32[40,128,512]{2,1,0:T(8,128)}, f32[40,128,512]{2,1,0:T(8,128)S(1)}, u32[]{:S(2)}, u32[]{:S(2)}) %collective-permute-start.1) | collective-permute-done | bytes 10485792 | tf_op jit(solution)/shard_map/ppermute | solution.py:9
  349.6 7.4 %collective-permute-done = f32[40,128,512]{2,1,0:T(8,128)} collective-permute-done((f32[40,128,512]{2,1,0:T(8,128)S(1)}, f32[40,128,512]{2,1,0:T(8,128)}, u32[]{:S(2)}, u32[]{:S(2)}) %collective-permute-start) | collective-permute-done | bytes 10485792 | tf_op jit(solution)/shard_map/ppermute | solution.py:9
  357.0 13.5 %fusion = f32[40,128,512]{2,1,0:T(8,128)} fusion(f32[40,128,512]{2,1,0:T(8,128)S(1)} %collective-permute-done.1, f32[40,128,512]{2,1,0:T(8,128)} %collective-permute-done, f32[120,128,512]{2,1,0:T(8,128)} %scatter_fusion), kind=kLoop, calls=%fused_computation.2 | loop fusion | flops 5242880 | bytes 41943040 | tf_op jit(solution)/shard_map/add | solution.py:41
  370.5 0.0 all-gather.2.cloned.1.call-update
  370.5 0.2 all-reduce.2.cloned.1.call-start
  370.7 32.1 %all-gather.2.cloned.1.call-done = f32[5120,1024]{1,0:T(8,128)} async-done(((f32[5120,512]{1,0:T(8,128)}), f32[5120,1024]{1,0:T(8,128)}) %all-gather.2.cloned.1.call-update) | async-done | bytes 20971536 | tf_op jit(solution)/shard_map/all_gather | solution.py:43
  402.8 0.0 copy-start.1
  402.8 21.4 %convolution_bitcast_fusion = f32[512,1024]{0,1:T(8,128)} fusion(f32[5120,1024]{1,0:T(8,128)} %all-gather.2.cloned.1.call-done, bf16[5120,512]{1,0:T(8,128)(2,1)} %param.5), kind=kOutput, calls=%fused_computation.4 | convolution fusion | flops 32212254720 | bytes 28311552 | tf_op jit(solution)/shard_map/dot_general | solution.py:14
  424.3 0.0 all-reduce.2.cloned.1.call-update
  424.3 134.1 %all-reduce.2.cloned.1.call-done = f32[512,1024]{0,1:T(8,128)} async-done(((f32[512,1024]{0,1:T(8,128)}), f32[512,1024]{0,1:T(8,128)}) %all-reduce.2.cloned.1.call-update) | async-done | bytes 2097168 | tf_op jit(solution)/shard_map/psum | solution.py:44
  558.4 1.4 dynamic-slice_multiply_fusion
  559.8 0.0 copy-done.1
Async XLA Ops:
  6.5 5.4 copy-start
  6.5 396.3 %all-gather.2.cloned.1.call-start = ((), (), s32[]{:S(2)}) async-start(), calls=%async_computation | async-start | bytes 31457280 | tf_op jit(solution)/shard_map/all_gather | solution.py:43
  116.0 233.6 %collective-permute-start.1 = (f32[40,128,512]{2,1,0:T(8,128)}, f32[40,128,512]{2,1,0:T(8,128)S(1)}, u32[]{:S(2)}, u32[]{:S(2)}) collective-permute-start(f32[40,128,512]{2,1,0:T(8,128)} %get-tuple-element.6), channel_id=1, source_target_pairs={{0,126},{2,0},{4,2},{6,4},{8,6},{10,8},{12,10},{14,12},{16,14},{18... | collective-permute-start | bytes 31457288 | tf_op jit(solution)/shard_map/ppermute | solution.py:9
  124.6 232.4 %collective-permute-start = (f32[40,128,512]{2,1,0:T(8,128)S(1)}, f32[40,128,512]{2,1,0:T(8,128)}, u32[]{:S(2)}, u32[]{:S(2)}) collective-permute-start(f32[40,128,512]{2,1,0:T(8,128)S(1)} %get-tuple-element.5), channel_id=1, source_target_pairs={{0,2},{2,4},{4,6},{6,8},{8,10},{10,12},{12,14},{14,16},{16,18},{18... | collective-permute-start | bytes 31457288 | tf_op jit(solution)/shard_map/ppermute | solution.py:9
  370.5 187.9 %all-reduce.2.cloned.1.call-start = ((), (), s32[]{:S(2)}) async-start(), calls=%async_computation.1 | async-start | bytes 4194304 | tf_op jit(solution)/shard_map/psum | solution.py:44
  402.8 156.9 %copy-start.1 = (bf16[80,128,128]{2,1,0:T(8,128)(2,1)S(1)}, bf16[80,128,128]{2,1,0:T(8,128)(2,1)}, u32[]{:S(2)}) copy-start(bf16[80,128,128]{2,1,0:T(8,128)(2,1)} %param.8) | copy-start | bytes 7864324
Sparse Core Ops, SparseCore 0:
  370.6 32.1 all-gather.1
  424.4 133.9 all-reduce.1
where the time goes:
time: 567 us
  waiting for transfers between devices  399 us (70%)
  other arithmetic  66.6 us (12%)
  local copies, waits for them, and re-layouts  49.1 us (9%)
  matrix products  30 us (5%)
  between operations  13.4 us (2%)
  starting transfers between devices  8.85 us (2%)
    ppermute x2, waiting for transfers between devices, shifted(): lax.ppermute(shard, axis, [(i, (i + by) % count) for i in range(count)])  232 us
    psum x1, waiting for transfers between devices, local(): totals = lax.psum(partial_grad, 'node')  134 us
    scatter-add x1, other arithmetic, local(): jnp.zeros((3 * blocks, tile_size, hslice), jnp.float32).at[tile_source]  46.3 us
    all_gather x1, waiting for transfers between devices, local(): lax.all_gather(summed, 'feat', axis=1, tiled=True)  32.1 us
    dot_general x1, matrix products, exact_product(): lax.dot_general(left_full, right_full, dims, precision=lax.Precision.HIGH...  21.4 us
    reshape x1, local copies, waits for them, and re-layouts, local(): contrib = contrib.reshape(blocks * tiles_each, tile_size, hslice)  21.4 us
    broadcast_in_dim x1, local copies, waits for them, and re-layouts, local(): jnp.zeros((3 * blocks, tile_size, hslice), jnp.float32).at[tile_source]  14.4 us
    add x1, other arithmetic, local(): buffer[blocks:2 * blocks] + from_lower + from_upper  13.5 us
  transfers between devices with their start and end apart: 4, of which 4 were waited for; matrix products, arithmetic and copies ran while one was open for 0% of the time, Pallas kernels for 0%

commit v1 on v0

v1 whole, which is shorter than its diff:
```python
import functools

import jax
import jax.numpy as jnp
from jax import lax
from jax.experimental import pallas as pl
from jax.experimental.pallas import tpu as pltpu
from jax.sharding import PartitionSpec as P

MESH = pl.DeviceIdType.MESH
SIDE = 4
TILE = 128
COLS = 128
ROWS = 512


def fused_kernel(cap, *refs):
    refs = list(refs)
    features, upstream, preact, adj_hbm, where, to_upper, to_lower, out = refs[:8]
    refs = refs[8:]
    stages = features.shape[2] // COLS
    own, refs = refs[:stages], refs[stages:]
    pool, refs = refs[:stages], refs[stages:]
    up_buf, refs = refs[:stages], refs[stages:]
    low_buf, refs = refs[:stages], refs[stages:]
    partial, refs = refs[:stages], refs[stages:]
    z_in, refs = refs[:stages], refs[stages:]
    z_sum, refs = refs[:stages], refs[stages:]
    y_in, refs = refs[:stages], refs[stages:]
    y_sum, refs = refs[:stages], refs[stages:]
    x_in, refs = refs[:stages], refs[stages:]
    (
        adj,
        grad_t,
        halves,
        up_rows,
        pre_rows,
        load_sem,
        adj_sem,
        row_sem,
        halo_send,
        halo_recv,
        core_send,
        core_recv,
        sum_send,
        sum_recv,
    ) = refs

    blocks = features.shape[0]
    hslice = upstream.shape[1]
    nodes = upstream.shape[0]
    row_steps = nodes // ROWS
    count = lax.axis_size("node")
    n, f = lax.axis_index("node"), lax.axis_index("feat")
    z, y, x = n // (SIDE * SIDE), (n // SIDE) % SIDE, n % SIDE
    upper, lower = lax.rem(n + 1, count), lax.rem(n + count - 1, count)

    def z_peer(d):
        return lax.rem(z + d, SIDE) * (SIDE * SIDE) + y * SIDE + x

    def y_peer(d):
        return z * (SIDE * SIDE) + lax.rem(y + d, SIDE) * SIDE + x

    def x_peer(d):
        return z * (SIDE * SIDE) + y * SIDE + lax.rem(x + d, SIDE)

    loads = []
    for k in range(stages):
        columns = features.at[:, :, pl.ds(k * COLS, COLS)]
        first = pltpu.make_async_copy(columns, own[k], load_sem.at[k, 0])
        second = pltpu.make_async_copy(columns, pool[k].at[pl.ds(cap, blocks)], load_sem.at[k, 1])
        first.start()
        loads.append((first, second))
    adj_load = pltpu.make_async_copy(adj_hbm, adj, adj_sem)

    def row_loads(step, slot):
        rows = pl.ds(pl.multiple_of(step * ROWS, ROWS), ROWS)
        return (
            pltpu.make_async_copy(upstream.at[rows], up_rows.at[slot], row_sem.at[slot, 0]),
            pltpu.make_async_copy(preact.at[rows], pre_rows.at[slot], row_sem.at[slot, 1]),
        )

    for copy in row_loads(0, 0):
        copy.start()
    adj_load.start()
    for k in range(stages):
        loads[k][1].start()

    barrier = pltpu.get_barrier_semaphore()
    greeted = [(upper, f), (lower, f), (n, 1 - f)]
    for d in range(1, SIDE):
        greeted += [(z_peer(d), f), (y_peer(d), f), (x_peer(d), f)]
    for target in greeted:
        pl.semaphore_signal(barrier, inc=1, device_id=target, device_id_type=MESH)

    def pack(k):
        loads[k][0].wait()

        def one(c, carry):
            up_buf[k][c] = own[k][to_upper[c]]
            low_buf[k][c] = own[k][to_lower[c]]
            return carry

        lax.fori_loop(0, cap, one, 0)

    def halo(k):
        return (
            pltpu.make_async_remote_copy(
                src_ref=up_buf[k],
                dst_ref=pool[k].at[pl.ds(0, cap)],
                send_sem=halo_send.at[k, 0],
                recv_sem=halo_recv.at[k, 0],
                device_id=(upper, f),
                device_id_type=MESH,
            ),
            pltpu.make_async_remote_copy(
                src_ref=low_buf[k],
                dst_ref=pool[k].at[pl.ds(cap + blocks, cap)],
                send_sem=halo_send.at[k, 1],
                recv_sem=halo_recv.at[k, 1],
                device_id=(lower, f),
                device_id_type=MESH,
            ),
        )

    halos = [halo(k) for k in range(stages)]
    pack(0)
    pl.semaphore_wait(barrier, len(greeted))
    for copy in halos[0]:
        copy.start()
    pack(1)
    for copy in halos[1]:
        copy.start()

    mine = pl.ds(pl.multiple_of(f * hslice, hslice), hslice)

    def core_copy(step):
        part = grad_t.at[mine, pl.ds(pl.multiple_of(step * ROWS, ROWS), ROWS)]
        return pltpu.make_async_remote_copy(
            src_ref=part,
            dst_ref=part,
            send_sem=core_send.at[step],
            recv_sem=core_recv.at[step],
            device_id=(n, 1 - f),
            device_id_type=MESH,
        )

    def mask_step(step, carry):
        slot = lax.rem(step, 2)

        @pl.when(step + 1 < row_steps)
        def _():
            for copy in row_loads(step + 1, 1 - slot):
                copy.start()

        for copy in row_loads(step, slot):
            copy.wait()
        kept = jnp.where(
            pre_rows[slot].astype(jnp.float32) > 0.0, up_rows[slot].astype(jnp.float32), 0.0
        )
        grad_t[mine, pl.ds(pl.multiple_of(step * ROWS, ROWS), ROWS)] = kept.astype(jnp.bfloat16).T
        core_copy(step).start()
        return carry

    lax.fori_loop(0, row_steps, mask_step, 0)
    adj_load.wait()
    for k in range(2, stages):
        pack(k)
    for k in range(stages):
        loads[k][1].wait()

    def core_wait(step, carry):
        core_copy(step).wait()
        return carry

    lax.fori_loop(0, row_steps, core_wait, 0)

    def sum_copy(k, phase, d, src, dst, target):
        return pltpu.make_async_remote_copy(
            src_ref=src,
            dst_ref=dst.at[d - 1],
            send_sem=sum_send.at[k, phase, d - 1],
            recv_sem=sum_recv.at[k, phase, d - 1],
            device_id=(target, f),
            device_id_type=MESH,
        )

    z_rows = partial[0].shape[0] // SIDE
    y_rows = z_rows // SIDE
    x_rows = y_rows // SIDE
    pending = []

    for k in range(stages):
        for copy in halos[k]:
            copy.wait_recv()
        if k + 2 < stages:
            for copy in halos[k + 2]:
                copy.start()

        def aggregate(b, carry):
            tiles = jnp.concatenate([adj[2 * b], adj[2 * b + 1]], axis=1)
            sources = jnp.concatenate([pool[k][where[2 * b]], pool[k][where[2 * b + 1]]], axis=0)
            total = jnp.dot(tiles, sources, preferred_element_type=jnp.float32)
            high = total.astype(jnp.bfloat16)
            low = (total - high.astype(jnp.float32)).astype(jnp.bfloat16)
            rows = pl.ds(pl.multiple_of(b * TILE, TILE), TILE)
            halves[rows, 0:COLS] = high
            halves[rows, COLS : 2 * COLS] = low
            return carry

        lax.fori_loop(0, blocks, aggregate, 0, unroll=4)

        z_copies = []
        for d in (2, 1, 3, 0):
            place = lax.rem(z + d, SIDE) * z_rows
            rows = pl.ds(pl.multiple_of(place, z_rows), z_rows)
            both = jnp.dot(grad_t[rows, :], halves[...], preferred_element_type=jnp.float32)
            partial[k][rows, :] = both[:, :COLS] + both[:, COLS:]
            if d:
                copy = sum_copy(k, 0, d, partial[k].at[rows], z_in[k], z_peer(d))
                copy.start()
                z_copies.append(copy)
        for copy in z_copies:
            copy.wait_recv()
        rows = pl.ds(pl.multiple_of(z * z_rows, z_rows), z_rows)
        z_sum[k][...] = partial[k][rows, :] + z_in[k][0] + z_in[k][1] + z_in[k][2]
        y_copies = []
        for d in (2, 1, 3):
            place = lax.rem(y + d, SIDE) * y_rows
            rows = pl.ds(pl.multiple_of(place, y_rows), y_rows)
            copy = sum_copy(k, 1, d, z_sum[k].at[rows], y_in[k], y_peer(d))
            copy.start()
            y_copies.append(copy)
        for copy in y_copies:
            copy.wait_recv()
        rows = pl.ds(pl.multiple_of(y * y_rows, y_rows), y_rows)
        y_sum[k][...] = z_sum[k][rows, :] + y_in[k][0] + y_in[k][1] + y_in[k][2]
        x_copies = []
        for d in (2, 1, 3):
            place = lax.rem(x + d, SIDE) * x_rows
            rows = pl.ds(pl.multiple_of(place, x_rows), x_rows)
            copy = sum_copy(k, 2, d, y_sum[k].at[rows], x_in[k], x_peer(d))
            copy.start()
            x_copies.append(copy)
        pending.append((z_copies + y_copies, x_copies))

    for k in range(stages):
        early, last = pending[k]
        for copy in last:
            copy.wait_recv()
        rows = pl.ds(pl.multiple_of(x * x_rows, x_rows), x_rows)
        out[:, k * COLS : (k + 1) * COLS] = y_sum[k][rows, :] + x_in[k][0] + x_in[k][1] + x_in[k][2]
        for copy in early + last:
            copy.wait_send()
        for copy in halos[k]:
            copy.wait_send()


def fused(cap, collective_id, features, upstream, preact, adj_tiles, where, to_upper, to_lower):
    nodes, fslice = features.shape
    hslice = upstream.shape[1]
    hidden = 2 * hslice
    blocks = nodes // TILE
    stages = fslice // COLS
    count = lax.axis_size("node")
    width = hidden // count
    f32, bf16 = jnp.float32, jnp.bfloat16

    def each(shape, dtype):
        return [pltpu.VMEM(shape, dtype)] * stages

    scratch = (
        each((blocks, TILE, COLS), bf16)
        + each((blocks + 2 * cap, TILE, COLS), bf16)
        + each((cap, TILE, COLS), bf16)
        + each((cap, TILE, COLS), bf16)
        + each((hidden, COLS), f32)
        + each((SIDE - 1, hidden // SIDE, COLS), f32)
        + each((hidden // SIDE, COLS), f32)
        + each((SIDE - 1, hidden // SIDE**2, COLS), f32)
        + each((hidden // SIDE**2, COLS), f32)
        + each((SIDE - 1, hidden // SIDE**3, COLS), f32)
        + [
            pltpu.VMEM(adj_tiles.shape, bf16),
            pltpu.VMEM((hidden, nodes), bf16),
            pltpu.VMEM((nodes, 2 * COLS), bf16),
            pltpu.VMEM((2, ROWS, hslice), bf16),
            pltpu.VMEM((2, ROWS, hslice), bf16),
            pltpu.SemaphoreType.DMA((stages, 2)),
            pltpu.SemaphoreType.DMA,
            pltpu.SemaphoreType.DMA((2, 2)),
            pltpu.SemaphoreType.DMA((stages, 2)),
            pltpu.SemaphoreType.DMA((stages, 2)),
            pltpu.SemaphoreType.DMA((nodes // ROWS,)),
            pltpu.SemaphoreType.DMA((nodes // ROWS,)),
            pltpu.SemaphoreType.DMA((stages, 3, SIDE - 1)),
            pltpu.SemaphoreType.DMA((stages, 3, SIDE - 1)),
        ]
    )
    in_hbm = pl.BlockSpec(memory_space=pl.ANY)
    in_smem = pl.BlockSpec(memory_space=pltpu.SMEM)
    flops = 4 * nodes * fslice * hidden + 4 * nodes * TILE * fslice
    return pl.pallas_call(
        functools.partial(fused_kernel, cap),
        out_shape=jax.ShapeDtypeStruct((width, fslice), f32),
        in_specs=[in_hbm] * 4 + [in_smem] * 3,
        out_specs=pl.BlockSpec(memory_space=pltpu.VMEM),
        scratch_shapes=scratch,
        cost_estimate=pl.CostEstimate(flops=flops, bytes_accessed=8 * nodes * fslice, transcendentals=0),
        compiler_params=pltpu.CompilerParams(
            collective_id=collective_id, has_side_effects=True, vmem_limit_bytes=62 * 1024 * 1024
        ),
    )(features.reshape(blocks, TILE, fslice), upstream, preact, adj_tiles, where, to_upper, to_lower)


def local(features, upstream, preact, adj_tiles, tile_source):
    nodes = features.shape[0]
    blocks = nodes // TILE
    factor = float(nodes * lax.axis_size("node")) ** (-0.5)
    order = jnp.arange(blocks, dtype=jnp.int32)
    summed = fused(blocks, 0, features, upstream, preact, adj_tiles, tile_source, order, order)
    return summed.T * factor


def solution(mesh):
    in_specs = (
        P("node", "feat"),
        P("node", "feat"),
        P("node", "feat"),
        P("node", None, None),
        P("node"),
    )
    out_specs = P("feat", "node")
    return jax.shard_map(local, mesh=mesh, in_specs=in_specs, out_specs=out_specs, check_vma=False)
```

time: 567 us -> 181 us (0.32)
  waiting for transfers between devices: 399 us -> 0 us
  Pallas kernels: 0 us -> 178 us
  other arithmetic: 66.6 us -> 1.38 us
  local copies, waits for them, and re-layouts: 49.1 us -> 1.05 us
  matrix products: 30 us -> 0 us
  between operations: 13.4 us -> 0.01 us
  starting transfers between devices: 8.85 us -> 0 us
    ppermute x2 -> x0, waiting for transfers between devices: 232 us -> none  [shifted(): lax.ppermute(shard, axis, [(i, (i + by) % count) for i in range(count)])]
    pallas_call x0 -> x1, Pallas kernels: none -> 178 us  [fused(): pl.pallas_call(functools.partial(fused_kernel, cap), out_shape=jax.ShapeD...]
    psum x1 -> x0, waiting for transfers between devices: 134 us -> none  [local(): totals = lax.psum(partial_grad, 'node')]
    scatter-add x1 -> x0, other arithmetic: 46.3 us -> none  [local(): jnp.zeros((3 * blocks, tile_size, hslice), jnp.float32).at[tile_source]]
    all_gather x1 -> x0, waiting for transfers between devices: 32.1 us -> none  [local(): lax.all_gather(summed, 'feat', axis=1, tiled=True)]
    dot_general x2 -> x0, matrix products: 30 us -> none  [the longest x1 21.4 us: exact_product(): lax.dot_general(left_full, right_full, dims, precision=lax.Precision.HIGH...]
    reshape x1 -> x0, local copies, waits for them, and re-layouts: 21.4 us -> none  [local(): contrib = contrib.reshape(blocks * tiles_each, tile_size, hslice)]
    broadcast_in_dim x1 -> x0, local copies, waits for them, and re-layouts: 14.4 us -> none  [local(): jnp.zeros((3 * blocks, tile_size, hslice), jnp.float32).at[tile_source]]
  transfers between devices with their start and end apart: 4 -> 0, of which waited for: 4 -> 0; matrix products, arithmetic and copies ran while one was open for 0% -> 0% of each run, Pallas kernels for 0% -> 0%
where the time goes in v1:
time: 181 us
  Pallas kernels  178 us (98%)
    pallas_call x1, Pallas kernels, fused(): pl.pallas_call(functools.partial(fused_kernel, cap), out_shape=jax.ShapeD...  178 us

profile of v1, /device:TPU:0, one launch (start us, length us, event | category | flops | bytes accessed | tf_op | source)
XLA Modules:
  0.0 180.7 jit_solution(1735926628626310559)
XLA Ops:
  0.0 0.5 iota.6.refs_6_
  0.5 0.5 iota.5.refs_5_
  1.1 178.3 %shard_map.55 = f32[16,512]{1,0:T(8,128)} custom-call(bf16[40,128,512]{2,1,0:T(8,128)(2,1)} %bitcast.3, bf16[5120,512]{1,0:T(8,128)(2,1)} %refs_1_.1, bf16[5120,512]{1,0:T(8,128)(2,1)} %refs_2_.1, bf16[80,128,128]{2,1,0:T(8,128)(2,1)} %refs_3_.1, s32[80]{0:T(128)} %refs_4_.1, s32[40]{0:T(128)} %iota.5.refs_5_, s32[40]{0:T(128)} %iota.6.refs_6_), custom_call_target="tpu_custom_call" | custom-call | flops 12079595520 | bytes 20971520 | tf_op jit(solution)/shard_map/pallas_call | solution.py:303
  179.3 1.4 multiply_bitcast_fusion

commit v2 on v1

v2 whole, which is shorter than its diff:
```python
import functools

import jax
import jax.numpy as jnp
from jax import lax
from jax.experimental import pallas as pl
from jax.experimental.pallas import tpu as pltpu
from jax.sharding import PartitionSpec as P

MESH = pl.DeviceIdType.MESH
SIDE = 4
TILE = 128
COLS = 128
ROWS = 512
LANES = 128
CAPACITY = 28
PARTS = ((0, 0, 16, (0, 1, 2)), (1, 0, 16, (1, 2, 0)), (2, 0, 16, (2, 0, 1)), (3, 0, 8, (0, 1, 2)), (3, 8, 8, (1, 2, 0)))


def request(cap, blocks, sources):
    row = lax.broadcasted_iota(jnp.int32, (LANES, LANES), 0)
    column = lax.broadcasted_iota(jnp.int32, (LANES, LANES), 1)
    wide = jnp.broadcast_to(sources, (LANES, LANES))
    named = jnp.where(row == wide, 1, 0)
    used = jnp.max(jnp.where(column == wide.T, 1, 0), axis=0, keepdims=True)

    def group(index):
        return jnp.where(index >= blocks, 1, 0) + jnp.where(index >= 2 * blocks, 1, 0)

    before = jnp.logical_and(column < row, group(column) == group(row))
    rank = jnp.sum(jnp.where(before, used, 0), axis=1, keepdims=True)
    marked = jnp.max(named, axis=1, keepdims=True)
    chosen = jnp.where(rank == column, marked, 0)
    lower_rows = row < blocks
    upper_rows = row >= 2 * blocks
    from_lower = jnp.sum(jnp.where(lower_rows, chosen * row, 0), axis=0, keepdims=True)
    from_upper = jnp.sum(jnp.where(upper_rows, chosen * (row - 2 * blocks), 0), axis=0, keepdims=True)
    held = jnp.minimum(rank, cap - 1)
    target = jnp.where(lower_rows, held, jnp.where(upper_rows, held + (cap + blocks), row + (cap - blocks)))
    where = jnp.sum(named * target, axis=0, keepdims=True)
    lower_count = jnp.sum(jnp.where(lower_rows, marked, 0), axis=0, keepdims=True)
    upper_count = jnp.sum(jnp.where(upper_rows, marked, 0), axis=0, keepdims=True)
    over = jnp.where(jnp.maximum(lower_count, upper_count) > cap, 1.0, 0.0)
    return from_lower, from_upper, where, over


def within(index, size):
    return jnp.minimum(jnp.maximum(index, 0), size - 1)


def fused_kernel(cap, *refs):
    refs = list(refs)
    features, upstream, preact, adj_hbm, sources, out, over = refs[:7]
    refs = refs[7:]
    stages = features.shape[2] // COLS
    own, refs = refs[:stages], refs[stages:]
    pool, refs = refs[:stages], refs[stages:]
    up_buf, refs = refs[:stages], refs[stages:]
    low_buf, refs = refs[:stages], refs[stages:]
    partial, refs = refs[:stages], refs[stages:]
    sums, refs = refs[: 5 * len(PARTS)], refs[5 * len(PARTS) :]
    flag_in, refs = refs[:3], refs[3:]
    flag, refs = refs[:3], refs[3:]
    (
        ask_lower,
        ask_upper,
        asked_by_upper,
        asked_by_lower,
        found,
        to_upper,
        to_lower,
        where,
        adj,
        grad_t,
        halves,
        up_rows,
        pre_rows,
        load_sem,
        adj_sem,
        row_sem,
        list_send,
        list_recv,
        list_local,
        flag_send,
        flag_recv,
        halo_send,
        halo_recv,
        core_send,
        core_recv,
        sum_send,
        sum_recv,
    ) = refs

    blocks = features.shape[0]
    tiles = sources.shape[1]
    hslice = upstream.shape[1]
    nodes = upstream.shape[0]
    row_steps = nodes // ROWS
    count = lax.axis_size("node")
    n, f = lax.axis_index("node"), lax.axis_index("feat")
    z, y, x = n // (SIDE * SIDE), (n // SIDE) % SIDE, n % SIDE
    upper, lower = lax.rem(n + 1, count), lax.rem(n + count - 1, count)

    def z_peer(d):
        return lax.rem(z + d, SIDE) * (SIDE * SIDE) + y * SIDE + x

    def y_peer(d):
        return z * (SIDE * SIDE) + lax.rem(y + d, SIDE) * SIDE + x

    def x_peer(d):
        return z * (SIDE * SIDE) + y * SIDE + lax.rem(x + d, SIDE)

    def remote(src, dst, send, recv, target):
        return pltpu.make_async_remote_copy(
            src_ref=src, dst_ref=dst, send_sem=send, recv_sem=recv, device_id=target, device_id_type=MESH
        )

    columns = [features.at[:, :, pl.ds(k * COLS, COLS)] for k in range(stages)]
    own_load = [pltpu.make_async_copy(columns[k], own[k], load_sem.at[k, 0]) for k in range(stages)]
    pool_load = [
        pltpu.make_async_copy(columns[k], pool[k].at[pl.ds(cap, blocks)], load_sem.at[k, 1]) for k in range(stages)
    ]
    adj_load = pltpu.make_async_copy(adj_hbm, adj, adj_sem)

    def row_loads(step, slot):
        rows = pl.ds(pl.multiple_of(step * ROWS, ROWS), ROWS)
        return (
            pltpu.make_async_copy(upstream.at[rows], up_rows.at[slot], row_sem.at[slot, 0]),
            pltpu.make_async_copy(preact.at[rows], pre_rows.at[slot], row_sem.at[slot, 1]),
        )

    own_load[0].start()
    own_load[1].start()
    for copy in row_loads(0, 0):
        copy.start()
    barrier = pltpu.get_barrier_semaphore()
    greeted = [(upper, f), (lower, f), (n, 1 - f)]
    for d in range(1, SIDE):
        greeted += [(z_peer(d), f), (y_peer(d), f), (x_peer(d), f)]
    for target in greeted:
        pl.semaphore_signal(barrier, inc=1, device_id=target, device_id_type=MESH)

    found[...] = jnp.full(found.shape, -1, jnp.int32)
    found[0:1, 0:tiles] = sources[...]
    from_lower, from_upper, spots, excess = request(cap, blocks, found[0:1, :])
    ask_lower[...] = jnp.broadcast_to(from_lower, ask_lower.shape)
    ask_upper[...] = jnp.broadcast_to(from_upper, ask_upper.shape)
    found[...] = jnp.broadcast_to(spots, found.shape)
    flag[0][...] = jnp.broadcast_to(excess, flag[0].shape)

    pl.semaphore_wait(barrier, len(greeted))
    ask = (
        remote(ask_lower, asked_by_upper, list_send.at[0], list_recv.at[0], (lower, f)),
        remote(ask_upper, asked_by_lower, list_send.at[1], list_recv.at[1], (upper, f)),
    )
    for copy in ask:
        copy.start()
    place_local = pltpu.make_async_copy(found, where, list_local.at[2])
    place_local.start()

    peers = (z_peer, y_peer, x_peer)
    position = (z, y, x)
    flags = [
        [
            remote(
                flag[phase],
                flag_in[phase].at[d - 1],
                flag_send.at[phase, d - 1],
                flag_recv.at[phase, d - 1],
                (peers[phase](d), f),
            )
            for d in range(1, SIDE)
        ]
        for phase in range(3)
    ]

    def flag_total(phase):
        for copy in flags[phase]:
            copy.wait_recv()
        return flag[phase][...] + flag_in[phase][0] + flag_in[phase][1] + flag_in[phase][2]

    ask[0].wait_recv()
    local_upper = pltpu.make_async_copy(asked_by_upper, to_upper, list_local.at[0])
    local_upper.start()
    ask[1].wait_recv()
    local_lower = pltpu.make_async_copy(asked_by_lower, to_lower, list_local.at[1])
    local_lower.start()
    local_upper.wait()
    local_lower.wait()

    halos = [
        (
            remote(up_buf[k], pool[k].at[pl.ds(0, cap)], halo_send.at[k, 0], halo_recv.at[k, 0], (upper, f)),
            remote(low_buf[k], pool[k].at[pl.ds(cap + blocks, cap)], halo_send.at[k, 1], halo_recv.at[k, 1], (lower, f)),
        )
        for k in range(stages)
    ]

    def pack(k):
        own_load[k].wait()

        def one(c, carry):
            up_buf[k][c] = own[k][within(to_upper[0, c], blocks)]
            low_buf[k][c] = own[k][within(to_lower[0, c], blocks)]
            return carry

        lax.fori_loop(0, cap, one, 0, unroll=2)

    for k in range(stages):
        pack(k)
        for copy in halos[k]:
            copy.start()
        if k == 0:
            for later in range(2, stages):
                own_load[later].start()
    adj_load.start()
    for k in range(stages):
        pool_load[k].start()

    mine = pl.ds(pl.multiple_of(f * hslice, hslice), hslice)

    def core_copy(step):
        part = grad_t.at[mine, pl.ds(pl.multiple_of(step * ROWS, ROWS), ROWS)]
        return remote(part, part, core_send.at[step], core_recv.at[step], (n, 1 - f))

    def mask_step(step, carry):
        slot = lax.rem(step, 2)

        @pl.when(step + 1 < row_steps)
        def _():
            for copy in row_loads(step + 1, 1 - slot):
                copy.start()

        for copy in row_loads(step, slot):
            copy.wait()
        kept = jnp.where(pre_rows[slot].astype(jnp.float32) > 0.0, up_rows[slot].astype(jnp.float32), 0.0)
        grad_t[mine, pl.ds(pl.multiple_of(step * ROWS, ROWS), ROWS)] = kept.astype(jnp.bfloat16).T
        core_copy(step).start()
        return carry

    lax.fori_loop(0, row_steps, mask_step, 0)
    adj_load.wait()
    for k in range(stages):
        pool_load[k].wait()

    def core_wait(step, carry):
        core_copy(step).wait()
        return carry

    lax.fori_loop(0, row_steps, core_wait, 0)
    place_local.wait()

    sent = []

    def buffers(i):
        first_in, first_sum, second_in, second_sum, third_in = sums[5 * i : 5 * i + 5]
        return (first_in, second_in, third_in), (None, first_sum, second_sum)

    def source(i, phase, place):
        stage, low, rows, order = PARTS[i]
        if phase == 0:
            spot = [slice(None)] * 3
            spot[order[0]] = place
            return partial[stage], tuple(spot) + (pl.ds(low, rows),)
        held = buffers(i)[1][phase]
        if phase == 1 and order[1] == max(order[1:]):
            return held, (slice(None), place)
        return held, (place,)

    arriving = {}

    def send(i, phase):
        axis = PARTS[i][3][phase]
        arriving[i] = []
        for d in (2, 1, 3):
            ref, spot = source(i, phase, lax.rem(position[axis] + d, SIDE))
            copy = remote(
                ref.at[spot],
                buffers(i)[0][phase].at[d - 1],
                sum_send.at[i, phase, d - 1],
                sum_recv.at[i, phase, d - 1],
                (peers[axis](d), f),
            )
            copy.start()
            arriving[i].append(copy)
        sent.extend(arriving[i])

    def total(i, phase):
        for copy in arriving[i]:
            copy.wait_recv()
        ref, spot = source(i, phase, position[PARTS[i][3][phase]])
        got = buffers(i)[0][phase]
        return ref[spot] + got[0] + got[1] + got[2]

    z_shape = partial[0].shape[1:]
    z_rows = z_shape[0] * z_shape[1] * z_shape[2]

    def multiply(k):
        def one(place, carry):
            rows = pl.ds(pl.multiple_of(place * z_rows, z_rows), z_rows)
            both = jnp.dot(grad_t[rows, :], halves[...], preferred_element_type=jnp.float32)
            partial[k][place] = (both[:, :COLS] + both[:, COLS:]).reshape(z_shape)
            return carry

        lax.fori_loop(0, SIDE, one, 0)

    for k in range(stages):
        for copy in halos[k]:
            copy.wait_recv()
        if k == stages - 1:
            for i in range(len(PARTS)):
                if PARTS[i][0] != k:
                    send(i, 0)
            for copy in flags[0]:
                copy.start()

        def aggregate(b, carry):
            pair = jnp.concatenate([adj[2 * b], adj[2 * b + 1]], axis=1)
            left = within(where[0, 2 * b], blocks + 2 * cap)
            right = within(where[0, 2 * b + 1], blocks + 2 * cap)
            inputs = jnp.concatenate([pool[k][left], pool[k][right]], axis=0)
            total = jnp.dot(pair, inputs, preferred_element_type=jnp.float32)
            high = total.astype(jnp.bfloat16)
            low = (total - high.astype(jnp.float32)).astype(jnp.bfloat16)
            rows = pl.ds(pl.multiple_of(b * TILE, TILE), TILE)
            halves[rows, 0:COLS] = high
            halves[rows, COLS : 2 * COLS] = low
            return carry

        lax.fori_loop(0, blocks, aggregate, 0, unroll=4)
        multiply(k)
    for i in range(len(PARTS)):
        if PARTS[i][0] == stages - 1:
            send(i, 0)
    for phase in (1, 2):
        for i in range(len(PARTS)):
            buffers(i)[1][phase][...] = total(i, phase - 1)
            send(i, phase)
        flag[phase][...] = flag_total(phase - 1)
        for copy in flags[phase]:
            copy.start()
    for i in range(len(PARTS)):
        stage, low, rows, _ = PARTS[i]
        out[low : low + rows, stage * COLS : (stage + 1) * COLS] = total(i, 2)
    over[...] = flag_total(2)
    for copy in sent:
        copy.wait_send()
    for pair in halos + [ask] + flags:
        for copy in pair:
            copy.wait_send()


def fused(cap, collective_id, features, upstream, preact, adj_tiles, sources):
    nodes, fslice = features.shape
    hslice = upstream.shape[1]
    hidden = 2 * hslice
    blocks = nodes // TILE
    stages = fslice // COLS
    width = hidden // lax.axis_size("node")
    f32, bf16, i32 = jnp.float32, jnp.bfloat16, jnp.int32
    peers = SIDE - 1
    steps = nodes // ROWS

    def each(shape, dtype, times=stages):
        return [pltpu.VMEM(shape, dtype)] * times

    def sems(*shape):
        return pltpu.SemaphoreType.DMA(shape)

    sums = []
    for _, _, rows, _ in PARTS:
        sums += [
            pltpu.VMEM((peers, SIDE, SIDE, rows, COLS), f32),
            pltpu.VMEM((SIDE, SIDE, rows, COLS), f32),
            pltpu.VMEM((peers, SIDE, rows, COLS), f32),
            pltpu.VMEM((SIDE, rows, COLS), f32),
            pltpu.VMEM((peers, rows, COLS), f32),
        ]

    scratch = (
        each((blocks, TILE, COLS), bf16)
        + each((blocks + 2 * cap, TILE, COLS), bf16)
        + each((cap, TILE, COLS), bf16)
        + each((cap, TILE, COLS), bf16)
        + each((SIDE, SIDE, SIDE, width, COLS), f32)
        + sums
        + each((peers, 8, LANES), f32, 3)
        + each((8, LANES), f32, 3)
        + each((8, LANES), i32, 5)
        + [pltpu.SMEM((8, LANES), i32)] * 3
        + [
            pltpu.VMEM(adj_tiles.shape, bf16),
            pltpu.VMEM((hidden, nodes), bf16),
            pltpu.VMEM((nodes, 2 * COLS), bf16),
            pltpu.VMEM((2, ROWS, hslice), bf16),
            pltpu.VMEM((2, ROWS, hslice), bf16),
            sems(stages, 2),
            pltpu.SemaphoreType.DMA,
            sems(2, 2),
            sems(2),
            sems(2),
            sems(3),
            sems(3, peers),
            sems(3, peers),
            sems(stages, 2),
            sems(stages, 2),
            sems(steps),
            sems(steps),
            sems(len(PARTS), 3, peers),
            sems(len(PARTS), 3, peers),
        ]
    )
    in_hbm = pl.BlockSpec(memory_space=pl.ANY)
    in_vmem = pl.BlockSpec(memory_space=pltpu.VMEM)
    flops = 4 * nodes * fslice * hidden + 4 * nodes * TILE * fslice
    return pl.pallas_call(
        functools.partial(fused_kernel, cap),
        out_shape=(jax.ShapeDtypeStruct((width, fslice), f32), jax.ShapeDtypeStruct((8, LANES), f32)),
        in_specs=[in_hbm] * 4 + [in_vmem],
        out_specs=(in_vmem, in_vmem),
        scratch_shapes=scratch,
        cost_estimate=pl.CostEstimate(flops=flops, bytes_accessed=8 * nodes * fslice, transcendentals=0),
        compiler_params=pltpu.CompilerParams(
            collective_id=collective_id, has_side_effects=True, vmem_limit_bytes=62 * 1024 * 1024
        ),
    )(features.reshape(blocks, TILE, fslice), upstream, preact, adj_tiles, sources)


def local(features, upstream, preact, adj_tiles, tile_source):
    nodes = features.shape[0]
    blocks = nodes // TILE
    factor = float(nodes * lax.axis_size("node")) ** (-0.5)
    args = (features, upstream, preact, adj_tiles, tile_source.reshape(1, -1))
    summed, over = fused(CAPACITY, 0, *args)
    summed = lax.cond(over[0, 0] > 0.0, lambda: fused(blocks, 1, *args)[0], lambda: summed)
    return summed.T * factor


def solution(mesh):
    in_specs = (
        P("node", "feat"),
        P("node", "feat"),
        P("node", "feat"),
        P("node", None, None),
        P("node"),
    )
    out_specs = P("feat", "node")
    return jax.shard_map(local, mesh=mesh, in_specs=in_specs, out_specs=out_specs, check_vma=False)
```

time: 181 us -> 122 us (0.67); the launches traced: 181 us -> 120 us
  Pallas kernels: 178 us -> 117 us
    pallas_call x1, Pallas kernels: 178 us -> 117 us  [fused(): pl.pallas_call(functools.partial(fused_kernel, cap), out_shape=(jax.Shape...]
where the time goes in v2:
time: 122 us; the launch traced here: 120 us
  Pallas kernels  117 us (96%)
    pallas_call x1, Pallas kernels, fused(): pl.pallas_call(functools.partial(fused_kernel, cap), out_shape=(jax.Shape...  117 us

profile of v2, /device:TPU:0, one launch (start us, length us, event | category | flops | bytes accessed | tf_op | source)
XLA Modules:
  0.0 119.8 jit_solution(2540765708148309974)
XLA Ops:
  0.0 0.0 copy-start
  0.0 117.3 %shard_map.55 = (f32[16,512]{1,0:T(8,128)S(1)}, f32[8,128]{1,0:T(8,128)}) custom-call(bf16[40,128,512]{2,1,0:T(8,128)(2,1)} %bitcast.6, bf16[5120,512]{1,0:T(8,128)(2,1)} %refs_1_.1, bf16[5120,512]{1,0:T(8,128)(2,1)} %refs_2_.1, bf16[80,128,128]{2,1,0:T(8,128)(2,1)} %refs_3_.1, s32[1,80]{1,0:T(1,128)} %bitcast.8), custom_call_target="tpu_custom_call" | custom-call | flops 12079595520 | bytes 20971520 | tf_op jit(solution)/shard_map/pallas_call | solution.py:416
  117.4 1.2 slice.3
  119.2 0.0 copy-done
  119.2 0.6 multiply_bitcast_fusion
  (1 shorter events, 0.0 us)
Async XLA Ops:
  0.0 119.2 %copy-start = (s32[80]{0:T(128)S(1)}, s32[80]{0:T(128)}, u32[]{:S(2)}) copy-start(s32[80]{0:T(128)} %param.11) | copy-start | bytes 964

commit v3 on v2

--- a/solution.py
+++ b/solution.py
@@ -17,7 +17,7 @@
 PARTS = ((0, 0, 16, (0, 1, 2)), (1, 0, 16, (1, 2, 0)), (2, 0, 16, (2, 0, 1)), (3, 0, 8, (0, 1, 2)), (3, 8, 8, (1, 2, 0)))
 
 
-def request(cap, blocks, sources):
+def request(skip, cap, blocks, sources):
     row = lax.broadcasted_iota(jnp.int32, (LANES, LANES), 0)
     column = lax.broadcasted_iota(jnp.int32, (LANES, LANES), 1)
     wide = jnp.broadcast_to(sources, (LANES, LANES))
@@ -30,17 +30,22 @@
     before = jnp.logical_and(column < row, group(column) == group(row))
     rank = jnp.sum(jnp.where(before, used, 0), axis=1, keepdims=True)
     marked = jnp.max(named, axis=1, keepdims=True)
-    chosen = jnp.where(rank == column, marked, 0)
+    chosen = jnp.where(rank == column + skip, marked, 0)
     lower_rows = row < blocks
     upper_rows = row >= 2 * blocks
     from_lower = jnp.sum(jnp.where(lower_rows, chosen * row, 0), axis=0, keepdims=True)
     from_upper = jnp.sum(jnp.where(upper_rows, chosen * (row - 2 * blocks), 0), axis=0, keepdims=True)
-    held = jnp.minimum(rank, cap - 1)
-    target = jnp.where(lower_rows, held, jnp.where(upper_rows, held + (cap + blocks), row + (cap - blocks)))
+    nothing = blocks + 2 * cap
+    slot = rank - skip
+    here = jnp.logical_and(slot >= 0, slot < cap)
+    lower_place = jnp.where(here, slot, nothing)
+    upper_place = jnp.where(here, slot + (cap + blocks), nothing)
+    own_place = nothing + 0 * row if skip else row + (cap - blocks)
+    target = jnp.where(lower_rows, lower_place, jnp.where(upper_rows, upper_place, own_place))
     where = jnp.sum(named * target, axis=0, keepdims=True)
     lower_count = jnp.sum(jnp.where(lower_rows, marked, 0), axis=0, keepdims=True)
     upper_count = jnp.sum(jnp.where(upper_rows, marked, 0), axis=0, keepdims=True)
-    over = jnp.where(jnp.maximum(lower_count, upper_count) > cap, 1.0, 0.0)
+    over = jnp.where(jnp.maximum(lower_count, upper_count) > skip + cap, 1.0, 0.0)
     return from_lower, from_upper, where, over
 
 
@@ -48,7 +53,7 @@
     return jnp.minimum(jnp.maximum(index, 0), size - 1)
 
 
-def fused_kernel(cap, *refs):
+def fused_kernel(skip, cap, *refs):
     refs = list(refs)
     features, upstream, preact, adj_hbm, sources, out, over = refs[:7]
     refs = refs[7:]
@@ -142,7 +147,7 @@
 
     found[...] = jnp.full(found.shape, -1, jnp.int32)
     found[0:1, 0:tiles] = sources[...]
-    from_lower, from_upper, spots, excess = request(cap, blocks, found[0:1, :])
+    from_lower, from_upper, spots, excess = request(skip, cap, blocks, found[0:1, :])
     ask_lower[...] = jnp.broadcast_to(from_lower, ask_lower.shape)
     ask_upper[...] = jnp.broadcast_to(from_upper, ask_upper.shape)
     found[...] = jnp.broadcast_to(spots, found.shape)
@@ -216,6 +221,7 @@
     adj_load.start()
     for k in range(stages):
         pool_load[k].start()
+        pool[k][blocks + 2 * cap] = jnp.zeros((TILE, COLS), jnp.bfloat16)
 
     mine = pl.ds(pl.multiple_of(f * hslice, hslice), hslice)
 
@@ -316,8 +322,8 @@
 
         def aggregate(b, carry):
             pair = jnp.concatenate([adj[2 * b], adj[2 * b + 1]], axis=1)
-            left = within(where[0, 2 * b], blocks + 2 * cap)
-            right = within(where[0, 2 * b + 1], blocks + 2 * cap)
+            left = within(where[0, 2 * b], blocks + 2 * cap + 1)
+            right = within(where[0, 2 * b + 1], blocks + 2 * cap + 1)
             inputs = jnp.concatenate([pool[k][left], pool[k][right]], axis=0)
             total = jnp.dot(pair, inputs, preferred_element_type=jnp.float32)
             high = total.astype(jnp.bfloat16)
@@ -327,7 +333,7 @@
             halves[rows, COLS : 2 * COLS] = low
             return carry
 
-        lax.fori_loop(0, blocks, aggregate, 0, unroll=4)
+        lax.fori_loop(0, blocks, aggregate, 0, unroll=8)
         multiply(k)
     for i in range(len(PARTS)):
         if PARTS[i][0] == stages - 1:
@@ -350,7 +356,7 @@
             copy.wait_send()
 
 
-def fused(cap, collective_id, features, upstream, preact, adj_tiles, sources):
+def fused(skip, cap, collective_id, features, upstream, preact, adj_tiles, sources):
     nodes, fslice = features.shape
     hslice = upstream.shape[1]
     hidden = 2 * hslice
@@ -379,7 +385,7 @@
 
     scratch = (
         each((blocks, TILE, COLS), bf16)
-        + each((blocks + 2 * cap, TILE, COLS), bf16)
+        + each((blocks + 2 * cap + 1, TILE, COLS), bf16)
         + each((cap, TILE, COLS), bf16)
         + each((cap, TILE, COLS), bf16)
         + each((SIDE, SIDE, SIDE, width, COLS), f32)
@@ -414,7 +420,7 @@
     in_vmem = pl.BlockSpec(memory_space=pltpu.VMEM)
     flops = 4 * nodes * fslice * hidden + 4 * nodes * TILE * fslice
     return pl.pallas_call(
-        functools.partial(fused_kernel, cap),
+        functools.partial(fused_kernel, skip, cap),
         out_shape=(jax.ShapeDtypeStruct((width, fslice), f32), jax.ShapeDtypeStruct((8, LANES), f32)),
         in_specs=[in_hbm] * 4 + [in_vmem],
         out_specs=(in_vmem, in_vmem),
@@ -431,8 +437,10 @@
     blocks = nodes // TILE
     factor = float(nodes * lax.axis_size("node")) ** (-0.5)
     args = (features, upstream, preact, adj_tiles, tile_source.reshape(1, -1))
-    summed, over = fused(CAPACITY, 0, *args)
-    summed = lax.cond(over[0, 0] > 0.0, lambda: fused(blocks, 1, *args)[0], lambda: summed)
+    summed, over = fused(0, CAPACITY, 0, *args)
+    summed = lax.cond(
+        over[0, 0] > 0.0, lambda: summed + fused(CAPACITY, blocks - CAPACITY, 1, *args)[0], lambda: summed
+    )
     return summed.T * factor
 
 

time: 122 us -> 187 us (1.53)
  Pallas kernels: 117 us -> 183 us
    pallas_call x1 -> x2, Pallas kernels: 117 us -> 183 us  [fused(): pl.pallas_call(functools.partial(fused_kernel, skip, cap), out_shape=(jax...]
where the time goes in v3:
time: 187 us
  Pallas kernels  183 us (98%)
    pallas_call x2, Pallas kernels, fused(): pl.pallas_call(functools.partial(fused_kernel, skip, cap), out_shape=(jax...  183 us

profile of v3, /device:TPU:0, one launch (start us, length us, event | category | flops | bytes accessed | tf_op | source)
XLA Modules:
  0.0 186.6 jit_solution(13482156400228902196)
XLA Ops:
  0.0 0.0 copy-start
  0.0 117.4 %shard_map.55 = (f32[16,512]{1,0:T(8,128)S(1)}, f32[8,128]{1,0:T(8,128)}) custom-call(bf16[40,128,512]{2,1,0:T(8,128)(2,1)} %bitcast.6, bf16[5120,512]{1,0:T(8,128)(2,1)} %refs_1_.1, bf16[5120,512]{1,0:T(8,128)(2,1)} %refs_2_.1, bf16[80,128,128]{2,1,0:T(8,128)(2,1)} %refs_3_.1, s32[1,80]{1,0:T(1,128)} %bitcast.8), custom_call_target="tpu_custom_call" | custom-call | flops 12079595520 | bytes 20971520 | tf_op jit(solution)/shard_map/pallas_call | solution.py:422
  117.4 1.2 slice.3
  119.2 0.0 copy-done
  119.2 66.7 %conditional.1 = (f32[16,512]{1,0:T(8,128)S(1)}) conditional(s32[]{:T(128)} %bitcast.3, f32[16,512]{1,0:T(8,128)S(1)} %get-tuple-element.31, (bf16[5120,512]{1,0:T(8,128)(2,1)}, bf16[5120,512]{1,0:T(8,128)(2,1)}, bf16[5120,512]{1,0:T(8,128)(2,1)}, bf16[80,128,128]{2,1,0:T(8,128)(2,1)}, s32[1,80]{1,0:T(1,128)S(1)}, ...), branch_computations={%region_0.0_spmd, %region_1.0_spmd} | conditional | flops 12079603712 | bytes 21069832 | solution.py:441
  119.3 65.9 %branch_1_fun.1 = (f32[16,512]{1,0:T(8,128)}, f32[8,128]{1,0:T(8,128)}) custom-call(bf16[40,128,512]{2,1,0:T(8,128)(2,1)} %bitcast.7, bf16[5120,512]{1,0:T(8,128)(2,1)} %get-tuple-element.23.refs_1_, bf16[5120,512]{1,0:T(8,128)(2,1)} %get-tuple-element.24.refs_2_, bf16[80,128,128]{2,1,0:T(8,128)(2,1)} %get-tuple-element.25.refs_3_, ...), custom_call_target="tpu_custom_call" | custom-call | flops 12079595520 | bytes 20971520 | tf_op jit(solution)/shard_map/cond/branch_1_fun/pallas_call | solution.py:422
  185.2 0.8 add.2
  186.0 0.6 multiply_bitcast_fusion
Async XLA Ops:
  0.0 119.2 %copy-start = (s32[80]{0:T(128)S(1)}, s32[80]{0:T(128)}, u32[]{:S(2)}) copy-start(s32[80]{0:T(128)} %param.11) | copy-start | bytes 964

commit v4 on v3

--- a/solution.py
+++ b/solution.py
@@ -348,7 +348,7 @@
     for i in range(len(PARTS)):
         stage, low, rows, _ = PARTS[i]
         out[low : low + rows, stage * COLS : (stage + 1) * COLS] = total(i, 2)
-    over[...] = flag_total(2)
+    over[0, 0] = jnp.max(flag_total(2))
     for copy in sent:
         copy.wait_send()
     for pair in halos + [ask] + flags:
@@ -421,9 +421,9 @@
     flops = 4 * nodes * fslice * hidden + 4 * nodes * TILE * fslice
     return pl.pallas_call(
         functools.partial(fused_kernel, skip, cap),
-        out_shape=(jax.ShapeDtypeStruct((width, fslice), f32), jax.ShapeDtypeStruct((8, LANES), f32)),
+        out_shape=(jax.ShapeDtypeStruct((width, fslice), f32), jax.ShapeDtypeStruct((1, 1), f32)),
         in_specs=[in_hbm] * 4 + [in_vmem],
-        out_specs=(in_vmem, in_vmem),
+        out_specs=(in_vmem, pl.BlockSpec(memory_space=pltpu.SMEM)),
         scratch_shapes=scratch,
         cost_estimate=pl.CostEstimate(flops=flops, bytes_accessed=8 * nodes * fslice, transcendentals=0),
         compiler_params=pltpu.CompilerParams(

time: 187 us -> 120 us (0.64)
  Pallas kernels: 183 us -> 117 us
    pallas_call x2 -> x1, Pallas kernels: 183 us -> 117 us  [fused(): pl.pallas_call(functools.partial(fused_kernel, skip, cap), out_shape=(jax...]
where the time goes in v4:
time: 120 us; the launch traced here: 119 us
  Pallas kernels  117 us (98%)
    pallas_call x1, Pallas kernels, fused(): pl.pallas_call(functools.partial(fused_kernel, skip, cap), out_shape=(jax...  117 us

profile of v4, /device:TPU:0, one launch (start us, length us, event | category | flops | bytes accessed | tf_op | source)
XLA Modules:
  0.0 118.7 jit_solution(14942370220248280139)
XLA Ops:
  0.0 0.0 copy-start
  0.0 117.4 %shard_map.55 = (f32[16,512]{1,0:T(8,128)S(1)}, f32[1,1]{1,0:T(1,128)}) custom-call(bf16[40,128,512]{2,1,0:T(8,128)(2,1)} %bitcast.6, bf16[5120,512]{1,0:T(8,128)(2,1)} %refs_1_.1, bf16[5120,512]{1,0:T(8,128)(2,1)} %refs_2_.1, bf16[80,128,128]{2,1,0:T(8,128)(2,1)} %refs_3_.1, s32[1,80]{1,0:T(1,128)} %bitcast.8), custom_call_target="tpu_custom_call" | custom-call | flops 12079595520 | bytes 20971520 | tf_op jit(solution)/shard_map/pallas_call | solution.py:422
  118.0 0.0 copy-done
  118.1 0.6 multiply_bitcast_fusion
  (1 shorter events, 0.0 us)
Async XLA Ops:
  0.0 118.0 %copy-start = (s32[80]{0:T(128)S(1)}, s32[80]{0:T(128)}, u32[]{:S(2)}) copy-start(s32[80]{0:T(128)} %param.11) | copy-start | bytes 964
